TPU v7x, 512 devices: a whole 4x8x8 slice. The times are simulated.
512 devices in a mesh: dp: 32 (over z_hi, y, core), ctx: 4 (over z_lo), rep: 4 (over x).
Axes of the slice: x: 4, y: 8, z: 8 (z_hi: 2, z_lo: 4; z = z_hi * 4 + z_lo), core: 2. Of those that a mesh axis runs over, the one named last changes fastest.
Arguments:
- tokens: bfloat16 [32768, 4096], P(('dp', 'rep'), 'ctx'), may hold values from -6 to 6
- cotangent: bfloat16 [32768, 4096], P(('dp', 'rep'), 'ctx'), may hold values from -6 to 6
- routes: int32 [32768, 8], P(('dp', 'rep')), may hold values from 0 to 127, all different within a row
- gates: float32 [32768, 8], P(('dp', 'rep')), may hold values from 0.05 to 0.6
- replica_of: int32 [2048], P(('dp', 'rep')), may hold values from 0 to 3
- capacity: int32 [32], replicated, may hold values from 1 to 2, as said below
- w_gate: bfloat16 [32, 4096, 768], P('dp', ('ctx', 'rep')), may hold values from -0.09375 to 0.09375
- w_up: bfloat16 [32, 4096, 768], P('dp', ('ctx', 'rep')), may hold values from -0.09375 to 0.09375
- w_down: bfloat16 [32, 768, 4096], P('dp', None, ('ctx', 'rep')), may hold values from -0.21875 to 0.21875
Outputs:
- layer_out: bfloat16 [32768, 4096], P(('dp', 'rep'), 'ctx')
- input_grad: bfloat16 [32768, 4096], P(('dp', 'rep'), 'ctx')
- grad_gate: bfloat16 [32, 4096, 768], P('dp', ('ctx', 'rep'))
- grad_up: bfloat16 [32, 4096, 768], P('dp', ('ctx', 'rep'))
- grad_down: bfloat16 [32, 768, 4096], P('dp', None, ('ctx', 'rep'))
Inputs may be any that keep to these rules, and one draw needn't show every extreme that they name: Some expert has capacity exactly 2.
All inputs are finite; a program needn't handle non-finite values.
Results may differ from a plain program's by a relative error of at most 0.029.
Values may be sent and summed in bfloat16 or wider, within the bound.
A program may use at most 128 MiB of HBM per device.

v0:
```python
import functools

import jax
import jax.numpy as jnp
from jax import lax
from jax.experimental import pallas as pl
from jax.experimental.pallas import tpu as pltpu
from jax.sharding import PartitionSpec as P

MESH = pl.DeviceIdType.MESH
BF = jnp.bfloat16
F32 = jnp.float32
BLK = 16
CAP = 2
LANES = 128
HID_CHUNKS = (384, 256, 128)
VMEM_BYTES = 58 * 1024 * 1024


def dot(left, right):
    return jnp.dot(left, right, preferred_element_type=F32)


def dot_first(left, right):
    return lax.dot_general(left, right, (((0,), (0,)), ((), ())), preferred_element_type=F32)


def dot_last(left, right):
    return lax.dot_general(left, right, (((1,), (1,)), ((), ())), preferred_element_type=F32)


def pack(stage, slot, rows, buckets, tiles):
    for tile in range(tiles):
        stage[pl.ds(slot * tiles + tile, buckets, stride=CAP * tiles), :] = rows[:, tile * LANES : (tile + 1) * LANES]


def unpack(stage, slot, tile, buckets, tiles):
    return stage[pl.ds(slot * tiles + tile, buckets, stride=CAP * tiles), :]


def expert_kernel(
    n_dp,
    n_ctx,
    n_rep,
    replica,
    capacity,
    routes,
    gates,
    tokens,
    cotangent,
    w_gate,
    w_up,
    w_down,
    layer_out,
    input_grad,
    grad_gate,
    grad_up,
    grad_down,
    token_rows,
    cotangent_rows,
    pick,
    pick_hi,
    pick_lo,
    leave,
    arrive,
    back_leave,
    back_arrive,
    all_gate,
    all_up,
    all_down,
    stage,
    rows,
    part,
    inbox,
    cross,
    act,
    total,
    grad_part,
    grad_relay,
    grad_in,
    out_rows,
    out_tall,
    out_wide,
    local_sem,
    row_sem,
    weight_sem,
    part_sem,
    act_sem,
    back_sem,
    relay_sem,
    grad_sem,
    out_sem,
):
    buckets = n_dp * n_rep
    my_dp, my_ctx, my_rep = (lax.axis_index(name) for name in ("dp", "ctx", "rep"))
    me = my_dp * n_rep + my_rep
    right, left = lax.rem(my_rep + 1, n_rep), lax.rem(my_rep + n_rep - 1, n_rep)
    beside = (right, left)
    across = lax.rem(my_rep + 2, n_rep)
    count, width = tokens.shape
    top = routes.shape[0]
    tiles = width // LANES
    piece = width // n_rep
    chunks = len(HID_CHUNKS)
    ends = [sum(HID_CHUNKS[: h + 1]) for h in range(chunks)]
    hid = [slice(end - size, end) for end, size in zip(ends, HID_CHUNKS)]
    share = rows.shape[1] // 2
    inner = jnp.logical_or(my_ctx == 1, my_ctx == 2)
    outer = jnp.logical_not(inner)
    partner = my_ctx + 1 - 2 * lax.rem(my_ctx, 2)
    opposite = n_ctx - 1 - my_ctx
    mine = pl.ds(pl.multiple_of((my_ctx // 2) * share, share), share)
    theirs = pl.ds(pl.multiple_of((1 - my_ctx // 2) * share, share), share)
    groups = (slice(0, 2), slice(2, 3))
    act_groups = (slice(0, 1), slice(1, 3))
    halves = (slice(0, piece // 2), slice(piece // 2, piece))

    def remote(source, target, sem, where):
        return pltpu.make_async_remote_copy(
            src_ref=source,
            dst_ref=target,
            send_sem=sem[0],
            recv_sem=sem[1],
            device_id=where,
            device_id_type=MESH,
        )

    def wait_for(view, sem):
        pltpu.make_async_copy(view, view, sem).wait()

    barrier = pltpu.get_barrier_semaphore()

    reps = [lax.rem(my_rep + step, n_rep) for step in range(n_rep)]

    def to_others(visit):
        def one(step, carry):
            other = lax.rem(my_dp + step, n_dp)
            for rep in reps:
                visit(other, rep)
            return carry

        lax.fori_loop(1, n_dp, one, 0)
        for rep in reps[1:]:
            visit(my_dp, rep)

    def greet(dp, rep):
        pl.semaphore_signal(barrier, inc=1, device_id={"dp": dp, "rep": rep}, device_id_type=MESH)

    with jax.named_scope("greet"):
        to_others(greet)
        for step in range(1, n_ctx):
            pl.semaphore_signal(
                barrier, inc=1, device_id={"ctx": lax.rem(my_ctx + step, n_ctx)}, device_id_type=MESH
            )
        loads = [
            pltpu.make_async_copy(source, target, local_sem.at[kind])
            for kind, (source, target) in enumerate(
                (
                    (tokens, token_rows),
                    (cotangent, cotangent_rows),
                    (w_gate, all_gate.at[my_rep]),
                    (w_up, all_up.at[my_rep]),
                    (w_down, all_down.at[my_rep]),
                )
            )
        ]
        for copy in loads:
            copy.start()

    with jax.named_scope("slots"):
        token = lax.broadcasted_iota(jnp.int32, (1, count), 1)
        serve = jnp.zeros((1, count), jnp.int32)
        for block in range(count // BLK):
            serve = jnp.where(token // BLK == block, replica[block], serve)
        bucket = lax.broadcasted_iota(jnp.int32, (buckets, 1), 0)
        limit = jnp.zeros((buckets, 1), jnp.int32)
        for expert in range(n_dp):
            limit = jnp.where(bucket // n_rep == expert, capacity[expert], limit)
        limit = limit.astype(F32)
        bucket = lax.broadcasted_iota(jnp.int32, (buckets, count), 0)
        earlier = jnp.where(
            lax.broadcasted_iota(jnp.int32, (count, count), 0) < lax.broadcasted_iota(jnp.int32, (count, count), 1),
            1.0,
            0.0,
        ).astype(BF)
        seen = jnp.zeros((buckets, 1), F32)
        kept = [jnp.zeros((buckets, count), F32) for _ in range(CAP)]
        weight = [jnp.zeros((buckets, count), F32) for _ in range(CAP)]
        for k in range(top):
            ones = jnp.where(bucket == routes[k : k + 1, :] * n_rep + serve, 1.0, 0.0)
            slot_of = dot(ones.astype(BF), earlier) + seen
            seen = seen + jnp.sum(ones, axis=1, keepdims=True)
            gate = gates[k : k + 1, :]
            for slot in range(CAP):
                here = jnp.where((slot_of == float(slot)) & (limit > float(slot)), ones, 0.0)
                kept[slot] = kept[slot] + here
                weight[slot] = weight[slot] + here * gate
        for slot in range(CAP):
            taken = slice(slot * buckets, (slot + 1) * buckets)
            high = weight[slot].astype(BF)
            pick[taken, :] = kept[slot].astype(BF)
            pick_hi[taken, :] = high
            pick_lo[taken, :] = (weight[slot] - high.astype(F32)).astype(BF)

    def gather(array):
        for slot in range(CAP):
            taken = slice(slot * buckets, (slot + 1) * buckets)
            if array == 0:
                picked = dot(pick[taken, :], token_rows[...])
            else:
                picked = dot(pick_hi[taken, :], cotangent_rows[...]) + dot(pick_lo[taken, :], cotangent_rows[...])
            pack(stage, slot, picked, buckets, tiles)
        leave[array] = stage[...].astype(BF).reshape(leave.shape[1:])

    with jax.named_scope("gather_rows"):
        for array in range(2):
            loads[array].wait()
            gather(array)

    weights = (
        (lambda h: w_gate.at[:, hid[h]], lambda q, h: all_gate.at[q, :, hid[h]]),
        (lambda h: w_up.at[:, hid[h]], lambda q, h: all_up.at[q, :, hid[h]]),
        (lambda h: w_down.at[hid[h], :], lambda q, h: all_down.at[q, hid[h], :]),
    )
    half_views = (
        lambda q, h, side: all_gate.at[q, halves[side], hid[h]],
        lambda q, h, side: all_up.at[q, halves[side], hid[h]],
        lambda q, h, side: all_down.at[
            q, slice(hid[h].start + side * HID_CHUNKS[h] // 2, hid[h].start + (side + 1) * HID_CHUNKS[h] // 2), :
        ],
    )

    def weight_copy(h, kind, side):
        source, target = weights[kind]
        return remote(
            source(h), target(my_rep, h), [weight_sem.at[h, kind, side, i] for i in range(2)], {"rep": beside[side]}
        )

    def relay_copy(h, kind, side):
        block = half_views[kind](beside[1 - side], h, side)
        return remote(block, block, [weight_sem.at[h, kind, side, 2 + i] for i in range(2)], {"rep": beside[side]})

    every = [(kind, side) for kind in range(3) for side in range(2)]

    def send_weights(h):
        for kind, side in every:
            weight_copy(h, kind, side).start()

    def relay_weights(h):
        for kind, side in every:
            weight_copy(h, kind, side).wait_recv()
            relay_copy(h, kind, side).start()

    def wait_weights(h, kinds):
        for kind in kinds:
            for side in range(2):
                relay_copy(h, kind, side).wait_recv()

    def exchange(source, target, sem):
        def send(dp, rep):
            remote(
                source.at[dp * n_rep + rep], target.at[me], (sem.at[0], sem.at[1]), {"dp": dp, "rep": rep}
            ).start()

        to_others(send)
        target[me] = source[me]

    def wait_exchange(target, sem):
        wait_for(target.at[pl.ds(0, buckets - 1)], sem)

    def take_rows(array):
        wait_exchange(arrive.at[array], row_sem.at[array, 1])
        stage[...] = arrive[array].astype(F32).reshape(stage.shape)
        for slot in range(CAP):
            for tile in range(tiles):
                rows[array, slot * buckets : (slot + 1) * buckets, tile * LANES : (tile + 1) * LANES] = unpack(
                    stage, slot, tile, buckets, tiles
                ).astype(BF)

    def part_copy(h, group, phase):
        source = (part.at[groups[group], theirs, hid[h]], part.at[groups[group], mine, hid[h]], cross.at[groups[group], :, hid[h]])
        return remote(
            source[phase],
            inbox.at[phase, groups[group], :, hid[h]],
            [part_sem.at[h, group, phase, i] for i in range(2)],
            {"ctx": opposite if phase == 2 else partner},
        )

    def send_part(h, group):
        if group == 0:
            for kind, full in enumerate((all_gate, all_up)):
                part[kind, :, hid[h]] = dot(rows[0], full[:, :, hid[h]].reshape(width, HID_CHUNKS[h])).astype(BF)
        else:
            part[2, :, hid[h]] = sum(
                dot_last(rows[1, :, q * piece : (q + 1) * piece], all_down[q, hid[h], :]) for q in range(n_rep)
            ).astype(BF)

        @pl.when(outer)
        def _():
            part_copy(h, group, 0).start()
            part_copy(h, group, 1).start()

    def cross_part(h, group):
        @pl.when(inner)
        def _():
            part_copy(h, group, 0).wait_recv()
            for kind in range(3)[groups[group]]:
                cross[kind, :, hid[h]] = (
                    part[kind, theirs, hid[h]].astype(F32) + inbox[0, kind, :, hid[h]].astype(F32)
                ).astype(BF)
            part_copy(h, group, 2).start()

    def summed(h, kind):
        return (
            part[kind, mine, hid[h]].astype(F32)
            + inbox[1, kind, :, hid[h]].astype(F32)
            + inbox[2, kind, :, hid[h]].astype(F32)
        )

    def act_copy(h, group, phase):
        block = act.at[act_groups[group], theirs if phase == 2 else mine, hid[h]]
        return remote(
            block,
            block,
            [act_sem.at[h, group, phase, i] for i in range(2)],
            {"ctx": opposite if phase == 0 else partner},
        )

    def activate(h, group):
        @pl.when(inner)
        def _():
            part_copy(h, group, 1).wait_recv()
            part_copy(h, group, 2).wait_recv()
            pre_gate, pre_up = summed(h, 0), summed(h, 1)
            sigmoid = jax.nn.sigmoid(pre_gate)
            swish = pre_gate * sigmoid
            if group == 0:
                act[0, mine, hid[h]] = (swish * pre_up).astype(BF)
            else:
                grad = summed(h, 2)
                act[1, mine, hid[h]] = (grad * pre_up * sigmoid * (1.0 + pre_gate * (1.0 - sigmoid))).astype(BF)
                act[2, mine, hid[h]] = (grad * swish).astype(BF)
            act_copy(h, group, 0).start()
            act_copy(h, group, 1).start()

    def relay_act(h, group):
        @pl.when(inner)
        def _():
            act_copy(h, group, 0).wait_recv()
            act_copy(h, group, 2).start()

    def wait_act(h, group):
        @pl.when(outer)
        def _():
            act_copy(h, group, 1).wait_recv()
            act_copy(h, group, 2).wait_recv()

    def add_outputs(h, array):
        for q in range(n_rep):
            columns = slice(q * piece, (q + 1) * piece)
            if array == 0:
                term = dot(act[0, :, hid[h]], all_down[q, hid[h], :])
            else:
                term = dot_last(act[1, :, hid[h]], all_gate[q, :, hid[h]]) + dot_last(
                    act[2, :, hid[h]], all_up[q, :, hid[h]]
                )
            total[array, :, columns] = term + total[array, :, columns] if h else term

    def send_outputs(array):
        for slot in range(CAP):
            pack(stage, slot, total[array, slot * buckets : (slot + 1) * buckets, :], buckets, tiles)
        back_leave[array] = stage[...].astype(BF).reshape(back_leave.shape[1:])
        exchange(back_leave.at[array], back_arrive.at[array], back_sem.at[array])

    def combine(array):
        wait_exchange(back_arrive.at[array], back_sem.at[array, 1])
        stage[...] = back_arrive[array].astype(F32).reshape(stage.shape)
        for tile in range(tiles):
            block = jnp.concatenate(
                [unpack(stage, slot, tile, buckets, tiles) for slot in range(CAP)], axis=0
            ).astype(BF)
            columns = slice(tile * LANES, (tile + 1) * LANES)
            if array == 0:
                out_rows[0, :, columns] = (dot_first(pick_hi[...], block) + dot_first(pick_lo[...], block)).astype(BF)
            else:
                out_rows[1, :, columns] = dot_first(pick[...], block).astype(BF)
        row_out(array).start()

    def row_out(array):
        return pltpu.make_async_copy(out_rows.at[array], (layer_out, input_grad)[array], out_sem.at[array])

    def grad_out(h, kind):
        source = (out_tall.at[0, :, hid[h]], out_tall.at[1, :, hid[h]], out_wide.at[hid[h], :])
        target = (grad_gate.at[:, hid[h]], grad_up.at[:, hid[h]], grad_down.at[hid[h], :])
        return pltpu.make_async_copy(source[kind], target[kind], out_sem.at[2 + 3 * h + kind])

    def grad_relay_copy(h, side):
        return remote(
            grad_part.at[across, :, halves[side], hid[h]],
            grad_relay.at[side, :, :, hid[h]],
            [relay_sem.at[h, side, i] for i in range(2)],
            {"rep": beside[side]},
        )

    def grad_copy(h, side):
        return remote(
            grad_part.at[beside[side], :, :, hid[h]],
            grad_in.at[side, :, :, hid[h]],
            [grad_sem.at[h, side, i] for i in range(2)],
            {"rep": beside[side]},
        )

    def make_grads(h):
        for q in range(n_rep):
            columns = slice(q * piece, (q + 1) * piece)
            for kind, (array, by) in enumerate(((0, 1), (0, 2), (1, 0))):
                grad_part[q, kind, :, hid[h]] = dot_first(rows[array, :, columns], act[by, :, hid[h]]).astype(BF)
        for side in range(2):
            grad_relay_copy(h, side).start()

    def pass_grads(h):
        for side in range(2):
            grad_relay_copy(h, side).wait_recv()
            grad_part[beside[side], :, halves[side], hid[h]] = (
                grad_part[beside[side], :, halves[side], hid[h]].astype(F32)
                + grad_relay[side, :, :, hid[h]].astype(F32)
            ).astype(BF)
            grad_copy(h, side).start()

    def add_grads(h):
        for side in range(2):
            grad_copy(h, side).wait_recv()
        for kind in range(3):
            full = (
                grad_part[my_rep, kind, :, hid[h]].astype(F32)
                + grad_in[0, kind, :, hid[h]].astype(F32)
                + grad_in[1, kind, :, hid[h]].astype(F32)
            )
            if kind < 2:
                out_tall[kind, :, hid[h]] = full.astype(BF)
            else:
                out_wide[hid[h], :] = full.T.astype(BF)
            grad_out(h, kind).start()

    with jax.named_scope("entry"):
        pl.semaphore_wait(barrier, buckets - 1 + n_ctx - 1)
    with jax.named_scope("issue"):
        send_weights(0)
        exchange(leave.at[0], arrive.at[0], row_sem.at[0])
        exchange(leave.at[1], arrive.at[1], row_sem.at[1])
        send_weights(1)
        send_weights(2)
        for copy in loads[2:]:
            copy.wait()

    def step(name, call, *args):
        with jax.named_scope(name):
            call(*args)

    def grads_and_outputs(h):
        wait_act(h, 0)
        wait_act(h, 1)
        make_grads(h)
        add_outputs(h, 0)
        add_outputs(h, 1)

    step("relay_0", relay_weights, 0)
    step("tokens", take_rows, 0)
    step("weights_0a", wait_weights, 0, (0, 1))
    step("part_0a", send_part, 0, 0)
    step("cross_0a", cross_part, 0, 0)
    step("relay_1", relay_weights, 1)
    step("scaled", take_rows, 1)
    step("weights_0b", wait_weights, 0, (2,))
    step("part_0b", send_part, 0, 1)
    step("activate_0a", activate, 0, 0)
    step("cross_0b", cross_part, 0, 1)
    step("relay_2", relay_weights, 2)
    step("weights_1", wait_weights, 1, (0, 1, 2))
    step("part_1a", send_part, 1, 0)
    step("part_1b", send_part, 1, 1)
    step("activate_0b", activate, 0, 1)
    step("act_0a", relay_act, 0, 0)
    step("cross_1a", cross_part, 1, 0)
    step("cross_1b", cross_part, 1, 1)
    step("act_0b", relay_act, 0, 1)
    step("activate_1a", activate, 1, 0)
    step("activate_1b", activate, 1, 1)
    step("weights_2", wait_weights, 2, (0, 1, 2))
    step("part_2a", send_part, 2, 0)
    step("part_2b", send_part, 2, 1)
    step("grads_0", grads_and_outputs, 0)
    step("act_1a", relay_act, 1, 0)
    step("act_1b", relay_act, 1, 1)
    step("cross_2a", cross_part, 2, 0)
    step("cross_2b", cross_part, 2, 1)
    step("grads_1", grads_and_outputs, 1)
    step("activate_2a", activate, 2, 0)
    step("activate_2b", activate, 2, 1)
    step("pass_0", pass_grads, 0)
    step("act_2a", relay_act, 2, 0)
    step("act_2b", relay_act, 2, 1)
    step("wait_2a", wait_act, 2, 0)
    step("outputs_a", add_outputs, 2, 0)
    step("return_a", send_outputs, 0)
    step("wait_2b", wait_act, 2, 1)
    step("outputs_b", add_outputs, 2, 1)
    step("return_b", send_outputs, 1)
    step("pass_1", pass_grads, 1)
    step("grads_2", make_grads, 2)
    step("add_0", add_grads, 0)
    step("pass_2", pass_grads, 2)
    step("add_1", add_grads, 1)
    step("combine_a", combine, 0)
    step("combine_b", combine, 1)
    step("add_2", add_grads, 2)

    with jax.named_scope("drain"):
        for array in range(2):
            wait_exchange(arrive.at[array], row_sem.at[array, 0])
            wait_exchange(back_arrive.at[array], back_sem.at[array, 0])
            row_out(array).wait()
        for h in range(chunks):
            for kind, side in every:
                weight_copy(h, kind, side).wait_send()
                relay_copy(h, kind, side).wait_send()
            for side in range(2):
                grad_relay_copy(h, side).wait_send()
                grad_copy(h, side).wait_send()
            for kind in range(3):
                grad_out(h, kind).wait()

        @pl.when(outer)
        def _():
            for h in range(chunks):
                for group in range(2):
                    for phase in range(2):
                        part_copy(h, group, phase).wait_send()

        @pl.when(inner)
        def _():
            for h in range(chunks):
                for group in range(2):
                    part_copy(h, group, 2).wait_send()
                    for phase in range(3):
                        act_copy(h, group, phase).wait_send()


def finish_kernel(*refs):
    count = (len(refs) - 1) // 2
    copies = [pltpu.make_async_copy(refs[i], refs[count + i], refs[-1].at[i]) for i in range(count)]
    for copy in copies:
        copy.start()
    for copy in copies:
        copy.wait()


def per_device(n_dp, n_ctx, n_rep, tokens, cotangent, routes, gates, replica_of, capacity, w_gate, w_up, w_down):
    count, width = tokens.shape
    buckets = n_dp * n_rep
    slots = CAP * buckets
    lines = CAP * (width // LANES)
    piece = width // n_rep
    hidden = w_gate.shape[2]
    chunks = len(HID_CHUNKS)
    vmem = pl.BlockSpec(memory_space=pltpu.VMEM)
    smem = pl.BlockSpec(memory_space=pltpu.SMEM)
    hbm = pl.BlockSpec(memory_space=pl.ANY)
    outs = (
        jax.ShapeDtypeStruct((count, width), BF),
        jax.ShapeDtypeStruct((count, width), BF),
        jax.ShapeDtypeStruct((piece, hidden), BF),
        jax.ShapeDtypeStruct((piece, hidden), BF),
        jax.ShapeDtypeStruct((hidden, piece), BF),
    )
    results = pl.pallas_call(
        functools.partial(expert_kernel, n_dp, n_ctx, n_rep),
        out_shape=outs,
        in_specs=[smem, smem, vmem, vmem, hbm, hbm, hbm, hbm, hbm],
        out_specs=[hbm] * 5,
        scratch_shapes=[
            pltpu.VMEM((count, width), BF),
            pltpu.VMEM((count, width), BF),
            pltpu.VMEM((slots, count), BF),
            pltpu.VMEM((slots, count), BF),
            pltpu.VMEM((slots, count), BF),
            pltpu.VMEM((2, buckets, lines, LANES), BF),
            pltpu.VMEM((2, buckets, lines, LANES), BF),
            pltpu.VMEM((2, buckets, lines, LANES), BF),
            pltpu.VMEM((2, buckets, lines, LANES), BF),
            pltpu.VMEM((n_rep, piece, hidden), BF),
            pltpu.VMEM((n_rep, piece, hidden), BF),
            pltpu.VMEM((n_rep, hidden, piece), BF),
            pltpu.VMEM((buckets * lines, LANES), F32),
            pltpu.VMEM((2, slots, width), BF),
            pltpu.VMEM((3, slots, hidden), BF),
            pltpu.VMEM((3, 3, slots // 2, hidden), BF),
            pltpu.VMEM((3, slots // 2, hidden), BF),
            pltpu.VMEM((3, slots, hidden), BF),
            pltpu.VMEM((2, slots, width), F32),
            pltpu.VMEM((n_rep, 3, piece, hidden), BF),
            pltpu.VMEM((2, 3, piece // 2, hidden), BF),
            pltpu.VMEM((2, 3, piece, hidden), BF),
            pltpu.VMEM((2, count, width), BF),
            pltpu.VMEM((2, piece, hidden), BF),
            pltpu.VMEM((hidden, piece), BF),
            pltpu.SemaphoreType.DMA((5,)),
            pltpu.SemaphoreType.DMA((2, 2)),
            pltpu.SemaphoreType.DMA((chunks, 3, 2, 4)),
            pltpu.SemaphoreType.DMA((chunks, 2, 3, 2)),
            pltpu.SemaphoreType.DMA((chunks, 2, 3, 2)),
            pltpu.SemaphoreType.DMA((2, 2)),
            pltpu.SemaphoreType.DMA((chunks, 2, 2)),
            pltpu.SemaphoreType.DMA((chunks, 2, 2)),
            pltpu.SemaphoreType.DMA((2 + 3 * chunks,)),
        ],
        compiler_params=pltpu.CompilerParams(
            vmem_limit_bytes=VMEM_BYTES, collective_id=0, has_side_effects=True
        ),
        name="experts",
    )(replica_of, capacity, routes.T, gates.T, tokens, cotangent, w_gate[0], w_up[0], w_down[0])
    layer_out, input_grad, grad_gate, grad_up, grad_down = pl.pallas_call(
        finish_kernel,
        out_shape=outs,
        in_specs=[vmem] * 5,
        out_specs=[hbm] * 5,
        scratch_shapes=[pltpu.SemaphoreType.DMA((5,))],
        name="finish",
    )(*results)
    return layer_out, input_grad, grad_gate[None], grad_up[None], grad_down[None]


def solution(mesh):
    rows = P(("dp", "rep"), "ctx")
    routed = P(("dp", "rep"), None)
    tall = P("dp", ("ctx", "rep"), None)
    wide = P("dp", None, ("ctx", "rep"))
    sizes = dict(mesh.shape)
    return jax.shard_map(
        functools.partial(per_device, sizes["dp"], sizes["ctx"], sizes["rep"]),
        mesh=mesh,
        in_specs=(rows, rows, routed, routed, P(("dp", "rep")), P(), tall, tall, wide),
        out_specs=(rows, rows, tall, tall, wide),
        check_vma=False,
    )
```

profile of v0, /device:TPU:2, one launch (start us, length us, event | category | flops | bytes accessed | tf_op | source)
XLA Modules:
  0.0 153.9 jit_solution(224169081689425180)
XLA Ops:
  0.6 150.1 %experts.1 = (bf16[256,1024]{1,0:T(8,128)(2,1)}, bf16[256,1024]{1,0:T(8,128)(2,1)}, bf16[256,768]{1,0:T(8,128)(2,1)}, bf16[256,768]{1,0:T(8,128)(2,1)}, bf16[768,256]{1,0:T(8,128)(2,1)}) custom-call(s32[16]{0:T(128)} %replica.1, s32[32]{0:T(128)} %capacity.1, s32[8,256]{1,0:T(8,128)} %bitcast.11, f32[8,256]{1,0:T(8,128)} %bitcast.12, ...), custom_call_target="tpu_custom_call" | custom-call | tf_op jit(solution)/shard_map/experts/pallas_call | solution.py:576
  150.8 2.9 %finish.1 = (bf16[256,1024]{1,0:T(8,128)(2,1)}, bf16[256,1024]{1,0:T(8,128)(2,1)}, bf16[256,768]{1,0:T(8,128)(2,1)}, bf16[256,768]{1,0:T(8,128)(2,1)}, bf16[768,256]{1,0:T(8,128)(2,1)}) custom-call(bf16[256,1024]{1,0:T(8,128)(2,1)} %get-tuple-element.15.refs_0_, bf16[256,1024]{1,0:T(8,128)(2,1)} %get-tuple-element.16.refs_1_, ...), custom_call_target="tpu_custom_call" | custom-call | tf_op jit(solution)/shard_map/finish/pallas_call | solution.py:622
where the time goes:
time: 154 us
  Pallas kernels  153 us (99%)
    pallas_call x1, Pallas kernels, per_device(): pl.pallas_call(functools.partial(expert_kernel, n_dp, n_ctx, n_rep), out_...  150 us

commit v1 on v0

--- a/solution.py
+++ b/solution.py
@@ -90,6 +90,7 @@
     relay_sem,
     grad_sem,
     out_sem,
+    column_sem,
 ):
     buckets = n_dp * n_rep
     my_dp, my_ctx, my_rep = (lax.axis_index(name) for name in ("dp", "ctx", "rep"))
@@ -147,7 +148,13 @@
         pl.semaphore_signal(barrier, inc=1, device_id={"dp": dp, "rep": rep}, device_id_type=MESH)
 
     with jax.named_scope("greet"):
-        to_others(greet)
+        def greet_column(step, carry):
+            greet(lax.rem(my_dp + step, n_dp), my_rep)
+            return carry
+
+        lax.fori_loop(1, n_dp, greet_column, 0)
+        for rep in reps[1:]:
+            greet(my_dp, rep)
         for step in range(1, n_ctx):
             pl.semaphore_signal(
                 barrier, inc=1, device_id={"ctx": lax.rem(my_ctx + step, n_ctx)}, device_id_type=MESH
@@ -212,11 +219,6 @@
             pack(stage, slot, picked, buckets, tiles)
         leave[array] = stage[...].astype(BF).reshape(leave.shape[1:])
 
-    with jax.named_scope("gather_rows"):
-        for array in range(2):
-            loads[array].wait()
-            gather(array)
-
     weights = (
         (lambda h: w_gate.at[:, hid[h]], lambda q, h: all_gate.at[q, :, hid[h]]),
         (lambda h: w_up.at[:, hid[h]], lambda q, h: all_up.at[q, :, hid[h]]),
@@ -443,13 +445,20 @@
             grad_out(h, kind).start()
 
     with jax.named_scope("entry"):
-        pl.semaphore_wait(barrier, buckets - 1 + n_ctx - 1)
+        pl.semaphore_wait(barrier, n_dp - 1 + n_rep - 1 + n_ctx - 1)
+    with jax.named_scope("first_weights"):
+        for rep in reps[1:]:
+            pl.semaphore_signal(column_sem, inc=1, device_id={"rep": rep}, device_id_type=MESH)
+        send_weights(0)
+    with jax.named_scope("gather_rows"):
+        for array in range(2):
+            loads[array].wait()
+            gather(array)
+
     with jax.named_scope("issue"):
-        send_weights(0)
+        pl.semaphore_wait(column_sem, n_rep - 1)
         exchange(leave.at[0], arrive.at[0], row_sem.at[0])
         exchange(leave.at[1], arrive.at[1], row_sem.at[1])
-        send_weights(1)
-        send_weights(2)
         for copy in loads[2:]:
             copy.wait()
 
@@ -465,11 +474,13 @@
         add_outputs(h, 1)
 
     step("relay_0", relay_weights, 0)
+    step("weights_to_1", send_weights, 1)
     step("tokens", take_rows, 0)
     step("weights_0a", wait_weights, 0, (0, 1))
     step("part_0a", send_part, 0, 0)
     step("cross_0a", cross_part, 0, 0)
     step("relay_1", relay_weights, 1)
+    step("weights_to_2", send_weights, 2)
     step("scaled", take_rows, 1)
     step("weights_0b", wait_weights, 0, (2,))
     step("part_0b", send_part, 0, 1)
@@ -484,20 +495,20 @@
     step("cross_1a", cross_part, 1, 0)
     step("cross_1b", cross_part, 1, 1)
     step("act_0b", relay_act, 0, 1)
-    step("activate_1a", activate, 1, 0)
-    step("activate_1b", activate, 1, 1)
     step("weights_2", wait_weights, 2, (0, 1, 2))
     step("part_2a", send_part, 2, 0)
     step("part_2b", send_part, 2, 1)
+    step("activate_1a", activate, 1, 0)
+    step("activate_1b", activate, 1, 1)
     step("grads_0", grads_and_outputs, 0)
+    step("cross_2a", cross_part, 2, 0)
+    step("cross_2b", cross_part, 2, 1)
     step("act_1a", relay_act, 1, 0)
     step("act_1b", relay_act, 1, 1)
-    step("cross_2a", cross_part, 2, 0)
-    step("cross_2b", cross_part, 2, 1)
-    step("grads_1", grads_and_outputs, 1)
     step("activate_2a", activate, 2, 0)
     step("activate_2b", activate, 2, 1)
     step("pass_0", pass_grads, 0)
+    step("grads_1", grads_and_outputs, 1)
     step("act_2a", relay_act, 2, 0)
     step("act_2b", relay_act, 2, 1)
     step("wait_2a", wait_act, 2, 0)
@@ -505,11 +516,11 @@
     step("return_a", send_outputs, 0)
     step("wait_2b", wait_act, 2, 1)
     step("outputs_b", add_outputs, 2, 1)
-    step("return_b", send_outputs, 1)
     step("pass_1", pass_grads, 1)
     step("grads_2", make_grads, 2)
+    step("return_b", send_outputs, 1)
+    step("pass_2", pass_grads, 2)
     step("add_0", add_grads, 0)
-    step("pass_2", pass_grads, 2)
     step("add_1", add_grads, 1)
     step("combine_a", combine, 0)
     step("combine_b", combine, 1)
@@ -613,6 +624,7 @@
             pltpu.SemaphoreType.DMA((chunks, 2, 2)),
             pltpu.SemaphoreType.DMA((chunks, 2, 2)),
             pltpu.SemaphoreType.DMA((2 + 3 * chunks,)),
+            pltpu.SemaphoreType.REGULAR,
         ],
         compiler_params=pltpu.CompilerParams(
             vmem_limit_bytes=VMEM_BYTES, collective_id=0, has_side_effects=True

time: 154 us -> 143 us (0.929)
  Pallas kernels: 153 us -> 142 us
    pallas_call x1, Pallas kernels: 150 us -> 139 us  [per_device(): pl.pallas_call(functools.partial(expert_kernel, n_dp, n_ctx, n_rep), out_...]
where the time goes in v1:
time: 143 us; the launch traced here: 142 us
  Pallas kernels  142 us (99%)
    pallas_call x1, Pallas kernels, per_device(): pl.pallas_call(functools.partial(expert_kernel, n_dp, n_ctx, n_rep), out_...  139 us
    pallas_call x1, Pallas kernels, per_device(): pl.pallas_call(finish_kernel, out_shape=outs, in_specs=[vmem] * 5, out_sp...  2.94 us

profile of v1, /device:TPU:2, one launch (start us, length us, event | category | flops | bytes accessed | tf_op | source)
XLA Modules:
  0.0 142.3 jit_solution(7373121766597920486)
XLA Ops:
  0.6 138.6 %experts.1 = (bf16[256,1024]{1,0:T(8,128)(2,1)}, bf16[256,1024]{1,0:T(8,128)(2,1)}, bf16[256,768]{1,0:T(8,128)(2,1)}, bf16[256,768]{1,0:T(8,128)(2,1)}, bf16[768,256]{1,0:T(8,128)(2,1)}) custom-call(s32[16]{0:T(128)} %replica.1, s32[32]{0:T(128)} %capacity.1, s32[8,256]{1,0:T(8,128)} %bitcast.11, f32[8,256]{1,0:T(8,128)} %bitcast.12, ...), custom_call_target="tpu_custom_call" | custom-call | tf_op jit(solution)/shard_map/experts/pallas_call | solution.py:587
  139.2 2.9 %finish.1 = (bf16[256,1024]{1,0:T(8,128)(2,1)}, bf16[256,1024]{1,0:T(8,128)(2,1)}, bf16[256,768]{1,0:T(8,128)(2,1)}, bf16[256,768]{1,0:T(8,128)(2,1)}, bf16[768,256]{1,0:T(8,128)(2,1)}) custom-call(bf16[256,1024]{1,0:T(8,128)(2,1)} %get-tuple-element.15.refs_0_, bf16[256,1024]{1,0:T(8,128)(2,1)} %get-tuple-element.16.refs_1_, ...), custom_call_target="tpu_custom_call" | custom-call | tf_op jit(solution)/shard_map/finish/pallas_call | solution.py:634

commit v2 on v1

--- a/solution.py
+++ b/solution.py
@@ -90,11 +90,9 @@
     relay_sem,
     grad_sem,
     out_sem,
-    column_sem,
 ):
     buckets = n_dp * n_rep
     my_dp, my_ctx, my_rep = (lax.axis_index(name) for name in ("dp", "ctx", "rep"))
-    me = my_dp * n_rep + my_rep
     right, left = lax.rem(my_rep + 1, n_rep), lax.rem(my_rep + n_rep - 1, n_rep)
     beside = (right, left)
     across = lax.rem(my_rep + 2, n_rep)
@@ -131,34 +129,22 @@
 
     barrier = pltpu.get_barrier_semaphore()
 
-    reps = [lax.rem(my_rep + step, n_rep) for step in range(n_rep)]
-
     def to_others(visit):
         def one(step, carry):
-            other = lax.rem(my_dp + step, n_dp)
-            for rep in reps:
-                visit(other, rep)
+            visit(lax.rem(my_dp + step, n_dp))
             return carry
 
         lax.fori_loop(1, n_dp, one, 0)
-        for rep in reps[1:]:
-            visit(my_dp, rep)
-
-    def greet(dp, rep):
-        pl.semaphore_signal(barrier, inc=1, device_id={"dp": dp, "rep": rep}, device_id_type=MESH)
+
+    def greet(where):
+        pl.semaphore_signal(barrier, inc=1, device_id=where, device_id_type=MESH)
 
     with jax.named_scope("greet"):
-        def greet_column(step, carry):
-            greet(lax.rem(my_dp + step, n_dp), my_rep)
-            return carry
-
-        lax.fori_loop(1, n_dp, greet_column, 0)
-        for rep in reps[1:]:
-            greet(my_dp, rep)
-        for step in range(1, n_ctx):
-            pl.semaphore_signal(
-                barrier, inc=1, device_id={"ctx": lax.rem(my_ctx + step, n_ctx)}, device_id_type=MESH
-            )
+        to_others(lambda dp: greet({"dp": dp}))
+        for rep in beside:
+            greet({"rep": rep})
+        for ctx in (partner, opposite):
+            greet({"ctx": ctx})
         loads = [
             pltpu.make_async_copy(source, target, local_sem.at[kind])
             for kind, (source, target) in enumerate(
@@ -259,16 +245,14 @@
                 relay_copy(h, kind, side).wait_recv()
 
     def exchange(source, target, sem):
-        def send(dp, rep):
-            remote(
-                source.at[dp * n_rep + rep], target.at[me], (sem.at[0], sem.at[1]), {"dp": dp, "rep": rep}
-            ).start()
+        def send(dp):
+            remote(source.at[dp], target.at[my_dp], (sem.at[0], sem.at[1]), {"dp": dp}).start()
 
         to_others(send)
-        target[me] = source[me]
+        target[my_dp] = source[my_dp]
 
     def wait_exchange(target, sem):
-        wait_for(target.at[pl.ds(0, buckets - 1)], sem)
+        wait_for(target.at[pl.ds(0, n_dp - 1)], sem)
 
     def take_rows(array):
         wait_exchange(arrive.at[array], row_sem.at[array, 1])
@@ -445,10 +429,8 @@
             grad_out(h, kind).start()
 
     with jax.named_scope("entry"):
-        pl.semaphore_wait(barrier, n_dp - 1 + n_rep - 1 + n_ctx - 1)
+        pl.semaphore_wait(barrier, n_dp - 1 + 4)
     with jax.named_scope("first_weights"):
-        for rep in reps[1:]:
-            pl.semaphore_signal(column_sem, inc=1, device_id={"rep": rep}, device_id_type=MESH)
         send_weights(0)
     with jax.named_scope("gather_rows"):
         for array in range(2):
@@ -456,7 +438,6 @@
             gather(array)
 
     with jax.named_scope("issue"):
-        pl.semaphore_wait(column_sem, n_rep - 1)
         exchange(leave.at[0], arrive.at[0], row_sem.at[0])
         exchange(leave.at[1], arrive.at[1], row_sem.at[1])
         for copy in loads[2:]:
@@ -595,10 +576,10 @@
             pltpu.VMEM((slots, count), BF),
             pltpu.VMEM((slots, count), BF),
             pltpu.VMEM((slots, count), BF),
-            pltpu.VMEM((2, buckets, lines, LANES), BF),
-            pltpu.VMEM((2, buckets, lines, LANES), BF),
-            pltpu.VMEM((2, buckets, lines, LANES), BF),
-            pltpu.VMEM((2, buckets, lines, LANES), BF),
+            pltpu.VMEM((2, n_dp, n_rep * lines, LANES), BF),
+            pltpu.VMEM((2, n_dp, n_rep * lines, LANES), BF),
+            pltpu.VMEM((2, n_dp, n_rep * lines, LANES), BF),
+            pltpu.VMEM((2, n_dp, n_rep * lines, LANES), BF),
             pltpu.VMEM((n_rep, piece, hidden), BF),
             pltpu.VMEM((n_rep, piece, hidden), BF),
             pltpu.VMEM((n_rep, hidden, piece), BF),
@@ -624,7 +605,6 @@
             pltpu.SemaphoreType.DMA((chunks, 2, 2)),
             pltpu.SemaphoreType.DMA((chunks, 2, 2)),
             pltpu.SemaphoreType.DMA((2 + 3 * chunks,)),
-            pltpu.SemaphoreType.REGULAR,
         ],
         compiler_params=pltpu.CompilerParams(
             vmem_limit_bytes=VMEM_BYTES, collective_id=0, has_side_effects=True

time: 143 us -> 125 us (0.87)
  the two profiles are of different devices: /device:TPU:2 before, /device:TPU:37 now
where the time goes in v2:
time: 125 us
  Pallas kernels  124 us (99%)
    pallas_call x1, Pallas kernels, per_device(): pl.pallas_call(functools.partial(expert_kernel, n_dp, n_ctx, n_rep), out_...  121 us
    pallas_call x1, Pallas kernels, per_device(): pl.pallas_call(finish_kernel, out_shape=outs, in_specs=[vmem] * 5, out_sp...  2.94 us

profile of v2, /device:TPU:37, one launch (start us, length us, event | category | flops | bytes accessed | tf_op | source)
XLA Modules:
  0.0 124.8 jit_solution(17457975145064031678)
XLA Ops:
  0.6 121.0 %experts.1 = (bf16[256,1024]{1,0:T(8,128)(2,1)}, bf16[256,1024]{1,0:T(8,128)(2,1)}, bf16[256,768]{1,0:T(8,128)(2,1)}, bf16[256,768]{1,0:T(8,128)(2,1)}, bf16[768,256]{1,0:T(8,128)(2,1)}) custom-call(s32[16]{0:T(128)} %replica.1, s32[32]{0:T(128)} %capacity.1, s32[8,256]{1,0:T(8,128)} %bitcast.11, f32[8,256]{1,0:T(8,128)} %bitcast.12, ...), custom_call_target="tpu_custom_call" | custom-call | tf_op jit(solution)/shard_map/experts/pallas_call | solution.py:568
  121.7 2.9 %finish.1 = (bf16[256,1024]{1,0:T(8,128)(2,1)}, bf16[256,1024]{1,0:T(8,128)(2,1)}, bf16[256,768]{1,0:T(8,128)(2,1)}, bf16[256,768]{1,0:T(8,128)(2,1)}, bf16[768,256]{1,0:T(8,128)(2,1)}) custom-call(bf16[256,1024]{1,0:T(8,128)(2,1)} %get-tuple-element.15.refs_0_, bf16[256,1024]{1,0:T(8,128)(2,1)} %get-tuple-element.16.refs_1_, ...), custom_call_target="tpu_custom_call" | custom-call | tf_op jit(solution)/shard_map/finish/pallas_call | solution.py:614

commit v3 on v2

--- a/solution.py
+++ b/solution.py
@@ -493,12 +493,12 @@
     step("act_2a", relay_act, 2, 0)
     step("act_2b", relay_act, 2, 1)
     step("wait_2a", wait_act, 2, 0)
+    step("wait_2b", wait_act, 2, 1)
+    step("grads_2", make_grads, 2)
     step("outputs_a", add_outputs, 2, 0)
     step("return_a", send_outputs, 0)
-    step("wait_2b", wait_act, 2, 1)
+    step("pass_1", pass_grads, 1)
     step("outputs_b", add_outputs, 2, 1)
-    step("pass_1", pass_grads, 1)
-    step("grads_2", make_grads, 2)
     step("return_b", send_outputs, 1)
     step("pass_2", pass_grads, 2)
     step("add_0", add_grads, 0)

time: 125 us -> 127 us (1.016)
  the two profiles are of different devices: /device:TPU:37 before, /device:TPU:33 now
where the time goes in v3:
time: 127 us
  Pallas kernels  126 us (99%)
    pallas_call x1, Pallas kernels, per_device(): pl.pallas_call(functools.partial(expert_kernel, n_dp, n_ctx, n_rep), out_...  123 us
    pallas_call x1, Pallas kernels, per_device(): pl.pallas_call(finish_kernel, out_shape=outs, in_specs=[vmem] * 5, out_sp...  2.94 us

profile of v3, /device:TPU:33, one launch (start us, length us, event | category | flops | bytes accessed | tf_op | source)
XLA Modules:
  0.0 126.7 jit_solution(16654364839319549173)
XLA Ops:
  0.6 122.9 %experts.1 = (bf16[256,1024]{1,0:T(8,128)(2,1)}, bf16[256,1024]{1,0:T(8,128)(2,1)}, bf16[256,768]{1,0:T(8,128)(2,1)}, bf16[256,768]{1,0:T(8,128)(2,1)}, bf16[768,256]{1,0:T(8,128)(2,1)}) custom-call(s32[16]{0:T(128)} %replica.1, s32[32]{0:T(128)} %capacity.1, s32[8,256]{1,0:T(8,128)} %bitcast.11, f32[8,256]{1,0:T(8,128)} %bitcast.12, ...), custom_call_target="tpu_custom_call" | custom-call | tf_op jit(solution)/shard_map/experts/pallas_call | solution.py:568
  123.6 2.9 %finish.1 = (bf16[256,1024]{1,0:T(8,128)(2,1)}, bf16[256,1024]{1,0:T(8,128)(2,1)}, bf16[256,768]{1,0:T(8,128)(2,1)}, bf16[256,768]{1,0:T(8,128)(2,1)}, bf16[768,256]{1,0:T(8,128)(2,1)}) custom-call(bf16[256,1024]{1,0:T(8,128)(2,1)} %get-tuple-element.15.refs_0_, bf16[256,1024]{1,0:T(8,128)(2,1)} %get-tuple-element.16.refs_1_, ...), custom_call_target="tpu_custom_call" | custom-call | tf_op jit(solution)/shard_map/finish/pallas_call | solution.py:614
